TPU v7x, 32 devices: a whole 2x2x4 slice. The times are simulated.
32 devices in a mesh: clip: 8 (over z, y), win: 4 (over x, core).
Axes of the slice: x: 2, y: 2, z: 4, core: 2. Of those that a mesh axis runs over, the one named last changes fastest.
Arguments:
- tokens: bfloat16 [16, 8, 392, 512], P('clip', 'win'), may hold values from -6 to 6
- cotangent: bfloat16 [16, 8, 392, 512], P('clip', 'win'), may hold values from -6 to 6
- adapter_ids: int32 [16], P('clip'), may hold values from 0 to 7, as said below
- ln1_gain: bfloat16 [512], P('clip'), may hold values from 0.5 to 1.5
- qkv_weight: bfloat16 [512, 1536], P('clip', 'win'), may hold values from -0.25 to 0.25
- qkv_bias: bfloat16 [1536], P('clip'), may hold values from -1.5 to 1.5
- proj_weight: bfloat16 [512, 512], P('clip', 'win'), may hold values from -2 to 2
- proj_bias: bfloat16 [512], P('clip'), may hold values from -1.5 to 1.5
- ln2_gain: bfloat16 [512], P('clip'), may hold values from 0.5 to 1.5
- fc1_weight: bfloat16 [512, 2048], P('clip', 'win'), may hold values from -0.25 to 0.25
- fc1_bias: bfloat16 [2048], P('clip'), may hold values from -1.5 to 1.5
- fc2_weight: bfloat16 [2048, 512], P('clip', 'win'), may hold values from -0.125 to 0.125
- fc2_bias: bfloat16 [512], P('clip'), may hold values from -1.5 to 1.5
- bias_table: bfloat16 [16, 2535], replicated, may hold values from -4 to 4
- qkv_down: bfloat16 [8, 512, 16], P('win', 'clip'), may hold values from -0.25 to 0.25
- qkv_up: bfloat16 [8, 16, 1536], P('win', None, 'clip'), may hold values from -0.75 to 0.75
- proj_down: bfloat16 [8, 512, 16], P('win', 'clip'), may hold values from -2 to 2
- proj_up: bfloat16 [8, 16, 512], P('win', None, 'clip'), may hold values from -0.75 to 0.75
- fc1_down: bfloat16 [8, 512, 16], P('win', 'clip'), may hold values from -0.25 to 0.25
- fc1_up: bfloat16 [8, 16, 2048], P('win', None, 'clip'), may hold values from -0.75 to 0.75
- fc2_down: bfloat16 [8, 2048, 16], P('win', 'clip'), may hold values from -0.125 to 0.125
- fc2_up: bfloat16 [8, 16, 512], P('win', None, 'clip'), may hold values from -0.75 to 0.75
Outputs:
- activations: bfloat16 [16, 8, 392, 512], P('clip', 'win')
- input_grad: bfloat16 [16, 8, 392, 512], P('clip', 'win')
- grad_qkv_down: float32 [8, 512, 16], P('win', 'clip')
- grad_qkv_up: float32 [8, 16, 1536], P('win', None, 'clip')
- grad_proj_down: float32 [8, 512, 16], P('win', 'clip')
- grad_proj_up: float32 [8, 16, 512], P('win', None, 'clip')
- grad_fc1_down: float32 [8, 512, 16], P('win', 'clip')
- grad_fc1_up: float32 [8, 16, 2048], P('win', None, 'clip')
- grad_fc2_down: float32 [8, 2048, 16], P('win', 'clip')
- grad_fc2_up: float32 [8, 16, 512], P('win', None, 'clip')
Inputs may be any that keep to these rules, and one draw needn't show every extreme that they name: `adapter_ids`: ids never fall from one clip to the next (clips are grouped by adapter); adapters 0 and 7 appear in every draw.
All inputs are finite; a program needn't handle non-finite values.
Results may differ from a plain program's by a relative error of at most 0.017.
Values may be sent and summed in bfloat16 or wider, within the bound.
A program may use at most 256 MiB of HBM per device.

v0:
```python
import functools
import jax
import jax.numpy as jnp
from jax import lax
from jax.experimental import pallas as pl
from jax.experimental.pallas import tpu as pltpu
from jax.sharding import PartitionSpec as P

BF = jnp.bfloat16
F32 = jnp.float32
NN = (((1,), (0,)), ((), ()))
NT = (((1,), (1,)), ((), ()))
TN = (((0,), (0,)), ((), ()))
LOG2E = 1.4426950408889634
LN2 = 0.6931471805599453
FAR = 1e9
VMEM_LIMIT = 60 * 2**20
TOK = 392
TOP = 208


def dot(left, right, dims):
    return lax.dot_general(left, right, dims, preferred_element_type=F32)


def lane_ids(shape):
    return lax.broadcasted_iota(jnp.int32, shape, len(shape) - 1)


def norm_stats(values):
    average = jnp.mean(values, axis=-1, keepdims=True)
    centred = values - average
    variance = jnp.mean(centred * centred, axis=-1, keepdims=True)
    inverse = lax.rsqrt(variance + 1e-05)
    return centred * inverse, inverse


def norm_back(gradient, gain, normed, inverse):
    scaled = gradient * gain
    centre = jnp.mean(scaled, axis=-1, keepdims=True)
    slope = jnp.mean(scaled * normed, axis=-1, keepdims=True)
    return inverse * (scaled - centre - normed * slope)


def add_rows(ref, n, at, value, first):
    @pl.when(first)
    def _():
        ref[n, :, at] = value

    @pl.when(jnp.logical_not(first))
    def _():
        ref[n, :, at] += value


MESH = pl.DeviceIdType.MESH


def enter(peers):
    barrier = pltpu.get_barrier_semaphore()
    for peer in peers:
        pl.semaphore_signal(barrier, inc=1, device_id=peer, device_id_type=MESH)
    pl.semaphore_wait(barrier, len(peers))


def remote(src, dst, send_sem, recv_sem, peer):
    return pltpu.make_async_remote_copy(
        src_ref=src,
        dst_ref=dst,
        send_sem=send_sem,
        recv_sem=recv_sem,
        device_id=peer,
        device_id_type=MESH,
    )


class Sender:
    def __init__(self, send_sem, recv_sem):
        self.send_sem, self.recv_sem, self.count = send_sem, recv_sem, 0

    def copy(self, src, dst, peer):
        n = self.count
        self.count += 1
        made = remote(src, dst, self.send_sem.at[n], self.recv_sem.at[n], peer)
        made.start()
        return made


def row_masks(rows):
    row = lax.broadcasted_iota(jnp.int32, (rows, 128), 0)
    return row < TOK // 2, row % 49 < 21, row % 7 < 3


def choose(mask, first, second):
    return jnp.concatenate(
        [
            jnp.where(mask, first[:, at : at + 128], second[:, at : at + 128])
            for at in range(0, first.shape[1], 128)
        ],
        axis=1,
    )


class Rows:
    def __init__(self, place, own, beside, mixed, tops, send_sem, recv_sem):
        self.place, self.own, self.beside, self.mixed, self.tops = place, own, beside, mixed, tops
        self.send_sem, self.recv_sem = send_sem, recv_sem
        self.items, self.rows, self.feats = own.shape

    def copy(self, kind, i):
        n = kind * self.items + i
        sems = self.send_sem.at[n], self.recv_sem.at[n]
        if kind == 0:
            return remote(self.own.at[i], self.beside.at[i], *sems, self.place.sibling)
        top = self.mixed.at[i, pl.ds(0, TOP)]
        return remote(top, self.tops.at[i], *sems, self.place.across)

    def begin(self, i):
        self.copy(0, i).start()

    def mix(self, i):
        self.copy(0, i).wait_recv()
        self.mixed[i] = choose(row_masks(self.rows)[1], self.beside[i], self.own[i])
        self.copy(1, i).start()

    def end(self, out, i):
        early, _, low_w = row_masks(self.rows)
        both = []
        for e in range(2):
            self.copy(1, i + e).wait_recv()
            top = choose(early[:TOP], self.tops[i + e], self.mixed[i + e, :TOP])
            both.append(jnp.concatenate([top, self.mixed[i + e, TOP:]], axis=0))
        for e in range(2):
            out[i + e] = choose(low_w, both[1 - e], both[e])

    def drain(self):
        for i in range(self.items):
            self.copy(0, i).wait_send()
            self.copy(1, i).wait_send()


class Place:
    def __init__(self, clip_size):
        self.c, self.w = lax.axis_index("clip"), lax.axis_index("win")
        self.z, self.y = self.c // 2, self.c % 2
        self.x, self.k = self.w // 2, self.w % 2
        self.zs = clip_size // 2
        self.sibling = (self.c, self.x * 2 + 1 - self.k)
        self.across = (self.c, (1 - self.x) * 2 + self.k)

    def clip_at(self, z_step, other_y):
        return (self.z + z_step + self.zs) % self.zs * 2 + (1 - self.y if other_y else self.y)

    def along_z(self, step):
        return (self.clip_at(step, False), self.w)

    def along_y(self):
        return (self.clip_at(0, True), self.w)


class Gather:
    COPIES = 29

    def __init__(self, place, unit, units, send_sem, recv_sem):
        self.place, self.unit, self.units = place, unit, units
        self.send_sem, self.recv_sem = send_sem, recv_sem
        self.hops = range(place.zs - 1)

    def make(self, kind, t=0):
        p, units = self.place, self.units
        kinds = ("up", "down", "y_up", "y_down", "s_up", "s_down", "sy_up", "sy_down")
        single = ("across", "own", "theirs", "y", "s_y")
        n = single.index(kind) if kind in single else 5 + 8 * t + kinds.index(kind)
        sems = self.send_sem.at[n], self.recv_sem.at[n]
        mine = units.at[p.k, p.c, p.x]
        if kind == "across":
            return remote(self.unit, mine, *sems, p.across)
        if kind == "own":
            return remote(self.unit, mine, *sems, p.sibling)
        if kind == "theirs":
            part = units.at[p.k, p.c, 1 - p.x]
        elif kind == "y":
            part = units.at[p.k, p.c]
        elif kind == "s_y":
            part = units.at[p.k, p.z * 2 + 1 - p.y]
        else:
            sign = -1 if kind.endswith("up") else 1
            far = p.z + sign * (t if kind in ("up", "down") else t + 1)
            part = units.at[p.k, far * 2 + (1 - p.y if kind.startswith("sy") else p.y)]
        if kind in ("up", "down"):
            peer = (p.c - 2 * sign, p.w)
        else:
            peer = p.along_y() if kind.startswith("y") else p.sibling
        return remote(part, part, *sems, peer)

    def when(self, kind, t, sending, act):
        p, last = self.place, self.place.zs - 1
        if kind.endswith("up"):
            holds = (p.z >= t) & (p.z < last) if sending and kind == "up" else p.z >= t + 1
        elif kind.endswith("down"):
            holds = (p.z <= last - t) & (p.z > 0) if sending and kind == "down" else p.z <= last - 1 - t
        else:
            act()
            return
        pl.when(holds)(act)

    def start(self, kind, t=0):
        self.when(kind, t, True, lambda: self.make(kind, t).start())

    def wait_recv(self, kind, t=0):
        self.when(kind, t, False, lambda: self.make(kind, t).wait_recv())

    def wait_send(self, kind, t=0):
        self.when(kind, t, True, lambda: self.make(kind, t).wait_send())

    def begin(self):
        self.start("across")
        self.start("own")

    def second(self):
        self.wait_recv("across")
        for kind in ("up", "down", "y", "theirs"):
            self.start(kind)

    def from_z(self, t):
        for way in ("up", "down"):
            self.wait_recv(way, t)
            if t + 1 in self.hops:
                self.start(way, t + 1)
            self.start("y_" + way, t)
            self.start("s_" + way, t)

    def from_y(self, t):
        if t < 0:
            self.wait_recv("y")
            self.start("s_y")
        else:
            for way in ("up", "down"):
                self.wait_recv("y_" + way, t)
                self.start("sy_" + way, t)

    def finish(self):
        for kind in ("own", "theirs", "s_y"):
            self.wait_recv(kind)
        for t in self.hops:
            for kind in ("s_up", "s_down", "sy_up", "sy_down"):
                self.wait_recv(kind, t)
        for kind in ("across", "own", "theirs", "y", "s_y"):
            self.wait_send(kind)
        for t in self.hops:
            for kind in ("up", "down", "y_up", "y_down", "s_up", "s_down", "sy_up", "sy_down"):
                self.wait_send(kind, t)


def pack_first(unit, vec, qkv_ref, qd_ref, qu_ref, ids_ref, vec_refs):
    unit[:, 0:384] = qkv_ref[...]
    for a in range(2):
        unit[16 * a : 16 * a + 16, 384:448] = qd_ref[a]
        unit[16 * a : 16 * a + 16, 448:512] = qu_ref[a, :, 0:64]
        unit[32 + 16 * a : 48 + 16 * a, 384:512] = qu_ref[a, :, 64:192]
    g1_ref, qb_ref, pb_ref, g2_ref, f1b_ref, f2b_ref = vec_refs
    vec[0:1, 0:64] = g1_ref[...].astype(F32)
    vec[0:1, 64:128] = qb_ref[:, 0:64].astype(F32)
    vec[1:2, :] = qb_ref[:, 64:192].astype(F32)
    vec[2:3, 0:64] = pb_ref[...].astype(F32)
    vec[2:3, 64:128] = g2_ref[...].astype(F32)
    vec[3:4, :] = f1b_ref[:, 0:128].astype(F32)
    vec[4:5, :] = f1b_ref[:, 128:256].astype(F32)
    vec[5:6, 0:64] = f2b_ref[...].astype(F32)
    vec[5:6, 64:128] = ids_ref[:, 0:64]
    vec[6:8, :] = jnp.zeros((2, 128), F32)


def unpack_vectors(vecs, outs):
    gain1, qkv_bias, proj_bias, gain2, fc1_bias, fc2_bias, ids = outs
    for c in range(vecs.shape[0]):
        v = vecs[c]
        short = slice(64 * c, 64 * c + 64)
        gain1[:, short] = v[0:1, 0:64]
        qkv_bias[:, 192 * c : 192 * c + 64] = v[0:1, 64:128]
        qkv_bias[:, 192 * c + 64 : 192 * c + 192] = v[1:2, :]
        proj_bias[:, short] = v[2:3, 0:64]
        gain2[:, short] = v[2:3, 64:128]
        fc1_bias[:, 256 * c : 256 * c + 128] = v[3:4, :]
        fc1_bias[:, 256 * c + 128 : 256 * c + 256] = v[4:5, :]
        fc2_bias[:, short] = v[5:6, 0:64]
        for n in range(2):
            ids[2 * c + n : 2 * c + n + 1, :] = jnp.broadcast_to(
                v[5:6, 64 + n : 65 + n], (1, ids.shape[1])
            )


def unpack_first(units, weight, down, up):
    for c in range(units.shape[1]):
        for n in range(4):
            unit = units.at[n % 2, c, n // 2]
            weight[64 * c : 64 * c + 64, 384 * n : 384 * n + 384] = unit[:, 0:384]
            for a in range(2):
                low = unit[16 * a : 16 * a + 16, 384:512]
                high = unit[32 + 16 * a : 48 + 16 * a, 384:512]
                down[2 * n + a, :, 64 * c : 64 * c + 64] = low[:, 0:64]
                up[2 * n + a, :, 192 * c : 192 * c + 64] = low[:, 64:128]
                up[2 * n + a, :, 192 * c + 64 : 192 * c + 192] = high


def pack_second(unit, refs):
    proj_ref, fc1_ref, fc2_ref, pd_ref, pu_ref, f1d_ref, f1u_ref, f2d_ref, f2u_ref = refs
    unit[0:64] = proj_ref[...]
    for t in range(4):
        unit[64 + 64 * t : 128 + 64 * t] = fc1_ref[:, 128 * t : 128 * t + 128]
    unit[320:576] = fc2_ref[...]
    for a in range(2):
        at = 576 + 16 * a
        unit[at : at + 16, 0:64] = pd_ref[a]
        unit[at : at + 16, 64:128] = pu_ref[a]
        unit[at + 32 : at + 48, 0:64] = f1d_ref[a]
        unit[at + 32 : at + 48, 64:128] = f2u_ref[a]
        for half in range(2):
            lanes = slice(128 * half, 128 * half + 128)
            unit[at + 64 + 32 * half : at + 80 + 32 * half] = f1u_ref[a, :, lanes]
            unit[at + 128 + 32 * half : at + 144 + 32 * half] = f2d_ref[a, :, lanes]


class Bias:
    def __init__(self, source, table, pairs, found, wide, select):
        self.source, self.table, self.pairs, self.found = source, table, pairs, found
        self.wide, self.select = wide, select
        self.heads = source.shape[0]

    def prepare(self):
        heads, pairs = self.heads, self.pairs
        pairs[...] = jnp.zeros(pairs.shape, BF)
        for a in range(15):
            pairs[a * heads : (a + 1) * heads, 0:169] = self.source[:, 169 * a : 169 * a + 169]

    def first(self, start, end):
        heads, pairs, found = self.heads, self.pairs, self.found
        lane = lane_ids((pairs.shape[1], 128))
        row = lax.broadcasted_iota(jnp.int32, (pairs.shape[1], 128), 0)
        query_at = (lane // 7 + 4) % 7 * 13 + (lane % 7 + 4) % 7
        wanted = jnp.where(lane < 49, row - query_at - 84, 10000)

        def one_key(key, carry):
            key_at = (key // 7 + 4) % 7 * 13 + (key % 7 + 4) % 7
            pick = jnp.where(wanted + key_at == 0, 1.0, 0.0).astype(BF)
            value = dot(pairs[...], pick, NN)
            for a in range(15):
                found[a, pl.ds(key, heads, stride=56), :] = value[a * heads : (a + 1) * heads]
            return carry

        lax.fori_loop(start, end, one_key, 0, unroll=2)

    def middle(self):
        for a in range(15):
            self.wide[:, 128 * a : 128 * a + 128] = self.found[a].astype(BF)
        row = lax.broadcasted_iota(jnp.int32, (128, TOK), 0)
        gap = lane_ids((128, TOK)) - row
        for t in range(8):
            self.select[128 * t : 128 * t + 128, :] = jnp.where(
                (gap == (t + 4) % 8 * 49) & (row < 49), 1.0, 0.0
            ).astype(BF)

    def last(self, blocks):
        for block in blocks:
            t = (block + 4) % 8
            value = dot(self.wide[:, (7 - t) * 128 : (15 - t) * 128], self.select[...], NN) * LOG2E
            for m in range(self.heads):
                self.table[m, 49 * block : 49 * block + 49, :] = value[56 * m : 56 * m + 49]


def attend_kernel(*refs, scale, per_group, width, per_clip, remote_size):
    if remote_size:
        tok_ref, source_ref, *refs = refs
        first_refs, vec_refs, refs = refs[:4], refs[4:10], refs[10:]
        dy_ref, second_refs, refs = refs[0], refs[1:10], refs[10:]
    else:
        x_ref, gain_ref, weight_ref, bias_ref, ids_ref, down_ref, up_ref, table_ref, *refs = refs
    probs_ref, out_ref, qkv_ref, reduced_ref, down_own, up_own, *refs = refs
    if remote_size:
        dy_out_ref, units_ref, x_ref, weight_ref, gain_ref, *vec_outs, ids_ref = refs[:10]
        refs = refs[10:]
    keys, queries, values_t, out_t, scores, table, table_sem, query_mask, *refs = refs
    group = pl.program_id(1)
    groups = pl.num_programs(1)
    item = pl.program_id(0)
    step = item * groups + group
    feats = x_ref.shape[-1]
    rows = x_ref.shape[1]

    if remote_size:
        bias_ref, down_ref, up_ref, unit1, vec, unit2, units1, vecs, *refs = refs
        bias = Bias(source_ref, table, *refs[:4])
        place = Place(remote_size)
        x_rows = Rows(place, tok_ref, *refs[4:9])
        dy_rows = Rows(place, dy_ref, *refs[9:14])
        gather1 = Gather(place, unit1, units1, *refs[14:16])
        gather2 = Gather(place, unit2, units_ref, *refs[16:18])
        vec_send, vec_recv, own_sem = refs[18:]
        items = dy_ref.shape[0]

        def vec_copy(d):
            to = ((place.c + d) % remote_size, place.w)
            return remote(vec, vecs.at[place.c], vec_send.at[d], vec_recv.at[d], to)

        @pl.when(step == 0)
        def _():
            pack_first(unit1, vec, *first_refs, vec_refs)
            pack_second(unit2, second_refs)
            mine = place.k, place.c, place.x
            units1[mine] = unit1[...]
            vecs[place.c] = vec[...]
            own = pltpu.make_async_copy(unit2, units_ref.at[mine], own_sem)
            own.start()
            enter(
                [place.sibling, place.across]
                + [((place.c + d) % remote_size, place.w) for d in range(1, remote_size)]
            )
            gather1.begin()
            for i in range(items):
                x_rows.begin(i)
            for d in range(1, remote_size):
                vec_copy(d).start()
            bias.prepare()
            gather1.second()
            pl.loop(0, items)(x_rows.mix)
            bias.first(0, 16)
            gather1.from_z(0)
            bias.first(16, 32)
            gather1.from_y(-1)
            gather1.from_z(1)
            bias.first(32, 50)
            gather1.from_y(0)
            gather1.from_z(2)
            bias.middle()
            gather1.from_y(1)
            bias.last(range(0, 4))
            gather1.from_y(2)
            own.wait()
            gather2.begin()
            bias.last(range(4, 8))
            for d in range(1, remote_size):
                vec_copy(d).wait_recv()
            unpack_vectors(vecs, (gain_ref, bias_ref, *vec_outs, ids_ref))
            gather1.finish()
            unpack_first(units1, weight_ref, down_ref, up_ref)
            x_rows.end(x_ref, 0)
            gather2.second()
            for d in range(1, remote_size):
                vec_copy(d).wait_send()

        @pl.when(step == 1)
        def _():
            for i in range(items):
                dy_rows.begin(i)

        @pl.when(step == 3)
        def _():
            pl.loop(0, items)(dy_rows.mix)

        for n in range(2, items, 2):

            @pl.when(step == 4 * n)
            def _():
                x_rows.end(x_ref, n)

        for t, at in enumerate((4, 8, 11)):

            @pl.when(step == at)
            def _():
                gather2.from_z(t)

        for t, at in ((-1, 5), (0, 9), (1, 12), (2, 15)):

            @pl.when(step == at)
            def _():
                gather2.from_y(t)

        @pl.when(step == 4 * items - 1)
        def _():
            for i in range(0, items, 2):
                dy_rows.end(dy_out_ref, i)
            gather2.finish()
            x_rows.drain()
            dy_rows.drain()

    else:

        def table_copy(g):
            at = pl.ds(g * per_group, per_group)
            return pltpu.make_async_copy(table_ref.at[at], table.at[at], table_sem.at[g])

        @pl.when(step == 0)
        def _():
            for g in range(table.shape[0] // per_group):
                table_copy(g).start()

    @pl.when((group == 0) & (item % per_clip == 0))
    def _():
        clip = item // per_clip
        if remote_size:
            clip = clip + place.c * 2
        ids = ids_ref[...]
        row = lax.broadcasted_iota(jnp.int32, ids.shape, 0)
        mine = jnp.sum(jnp.where(row == clip, ids, 0.0), axis=0, keepdims=True)[:, 0:1]
        for ref, target in ((down_ref, down_own), (up_ref, up_own)):
            total = jnp.zeros(ref.shape[1:], F32)
            for a in range(ref.shape[0]):
                total = total + jnp.where(
                    mine == float(a), ref[a].astype(F32), 0.0
                )
            target[0] = total.astype(BF)

    @pl.when(group == 0)
    def _():
        number = lax.axis_index("win") * per_clip + item % per_clip
        early, low_h, low_w = row_masks(rows)
        label = (
            jnp.where(early, number // 4 % 2 * 4, 0)
            + jnp.where(low_h, number // 2 % 2 * 2, 0)
            + jnp.where(low_w, number % 2, 0)
        )
        lane = lane_ids((rows, 128))
        same = label == lane
        key_mask = jnp.where(same, 1.0, 0.0).astype(BF)
        query_mask[...] = jnp.where(same | (lane >= 8), 0.0, -FAR).astype(BF)
        normed, _ = norm_stats(x_ref[item if remote_size else 0].astype(F32))
        low = (normed * gain_ref[...]).astype(BF)
        reduced = dot(down_own[0], low, NT).astype(BF)
        reduced_ref[0] = reduced

        def columns(part):
            at = pl.ds(part * feats, feats)
            return (
                dot(low, weight_ref[:, at], NN)
                + bias_ref[:, at]
                + dot(reduced, up_own[0, :, at], TN)
            )

        query = (columns(0) * (scale * LOG2E)).astype(BF)
        queries[...] = query
        qkv_ref[0, :, :feats] = query
        key = columns(1).astype(BF)
        qkv_ref[0, :, feats : 2 * feats] = key
        for g in range(feats // 128):
            keys[:, 256 * g : 256 * g + 128] = key[:, 128 * g : 128 * g + 128]
            keys[:, 256 * g + 128 : 256 * g + 256] = key_mask
        value = columns(2).astype(BF)
        qkv_ref[0, :, 2 * feats :] = value
        values_t[...] = value.T

    if not remote_size:

        @pl.when(item == 0)
        def _():
            table_copy(group).wait()

    keys_now = keys[:, pl.ds(pl.multiple_of(group * 256, 256), 256)]
    query_now = queries[:, pl.ds(pl.multiple_of(group * 128, 128), 128)]
    head_of_lane = lane_ids(query_now.shape) // width

    def raw(h):
        own = jnp.where(head_of_lane == h, query_now, jnp.zeros_like(query_now))
        own = jnp.concatenate([own, query_mask[...]], axis=1)
        return dot(keys_now, own, NT) + table[group * per_group + h]

    def finish(h):
        score = scores[h % 2]
        largest = jnp.max(score, axis=0, keepdims=True)
        probs = jnp.exp2(score - largest)
        total = jnp.sum(probs, axis=0, keepdims=True)
        probs = (probs * (1.0 / total)).astype(BF)
        probs_ref[0, h] = probs
        at = pl.ds(pl.multiple_of((group * per_group + h) * width, width), width)
        out_t[at, :] = dot(values_t[at, :], probs, NN).astype(BF)

    scores[0] = raw(0)
    for h in range(per_group):
        if h + 1 < per_group:
            scores[(h + 1) % 2] = raw(h + 1)
        finish(h)

    @pl.when(group == groups - 1)
    def _():
        out_ref[0] = out_t[...].T


def dense_kernel(
    ids_ref,
    x_ref,
    attn_ref,
    gain_ref,
    proj_bias_ref,
    fc1_bias_ref,
    fc2_bias_ref,
    dy_ref,
    staged_ref,
    *refs,
    per_clip,
    chunk,
):
    tiles, refs = refs[:6], refs[6:]
    act_ref, dx1_ref, dattn_ref, grad_ref, *refs = refs
    proj_ref, fc1_ref, fc2_ref, proj_down, proj_up, fc1_down, fc1_up, fc2_down, fc2_up, *refs = refs
    pres, acts, dpres, sem = refs
    starting = pl.program_id(0) == 0
    count = x_ref.shape[1]
    feats = x_ref.shape[-1]
    hidden = fc1_ref.shape[-1]

    def moves(first=0, last=24):
        found = [(0, 64, proj_ref, 128 * n, n) for n in range(4)]
        found += [(64 + 64 * t, 64, fc1_ref, 512 * n + 128 * t, n) for n in range(4) for t in range(4)]
        found += [(320, 256, fc2_ref, 128 * n, n) for n in range(4)]
        return [
            pltpu.make_async_copy(
                staged_ref.at[n % 2, :, n // 2, pl.ds(start, size), :],
                target.at[:, :, pl.ds(lane, 128)],
                sem.at[at],
            )
            for at, (start, size, target, lane, n) in enumerate(found)
            if first <= at < last
        ]

    def arrive(first, last):
        @pl.when(starting)
        def _():
            for copy in moves(first, last):
                copy.wait()

    @pl.when(starting)
    def _():
        for copy in moves():
            copy.start()

    for n in range(8):
        short = slice(64 * n, 64 * n + 64)
        proj_down[:, short] = tiles[0][0, n, 0, :, 0:64]
        proj_up[:, short] = tiles[0][0, n, 0, :, 64:128]
        fc1_down[:, short] = tiles[1][0, n, 0, :, 0:64]
        fc2_up[:, short] = tiles[1][0, n, 0, :, 64:128]
        for half in range(2):
            long = slice(256 * n + 128 * half, 256 * n + 128 * half + 128)
            fc1_up[:, long] = tiles[2 + half][0, n, 0]
            fc2_down[:, long] = tiles[4 + half][0, n, 0]

    def join(parts):
        return jnp.concatenate(parts, axis=0) if per_clip > 1 else parts[0]

    dy = join([dy_ref[e] for e in range(per_clip)])
    attn = join([attn_ref[e] for e in range(per_clip)])
    reduced_proj = dot(proj_down[...], attn, NT).astype(BF)
    arrive(0, 4)
    proj_w = proj_ref[...].reshape(feats, feats)
    middle = (
        join([x_ref[e].astype(F32) for e in range(per_clip)])
        + dot(attn, proj_w, NN)
        + proj_bias_ref[...]
        + dot(reduced_proj, proj_up[...], TN)
    )
    normed, inverse = norm_stats(middle)
    low = (normed * gain_ref[...]).astype(BF)
    reduced_fc1 = dot(fc1_down[...], low, NT).astype(BF)
    grad_reduced_fc2 = dot(fc2_up[...], dy, NT).astype(BF)
    per_chunk = chunk // fc2_ref.shape[1]
    steps = hidden // chunk

    def pre_of(j):
        at = slice(j * chunk, (j + 1) * chunk)
        pres[j % 2] = (
            dot(low, fc1_ref[:, :, at].reshape(feats, chunk), NN)
            + fc1_bias_ref[:, at]
            + dot(reduced_fc1, fc1_up[:, at], TN)
        )

    arrive(4, 20)
    pre_of(0)
    arrive(20, 24)
    for j in range(steps):
        at = slice(j * chunk, (j + 1) * chunk)
        if j + 1 < steps:
            pre_of(j + 1)
        fc2_w = fc2_ref[j * per_chunk : (j + 1) * per_chunk].reshape(chunk, feats)
        dact = dot(dy, fc2_w, NT) + dot(grad_reduced_fc2, fc2_down[:, at], TN)
        pre = pres[j % 2]
        bell = jnp.exp2((pre * pre) * (-0.5 * LOG2E))
        t = 1.0 / (1.0 + jnp.abs(pre) * (0.3275911 * 0.7071067811865476))
        poly = (
            (((0.5 * 1.061405429) * t - 0.5 * 1.453152027) * t + 0.5 * 1.421413741) * t
            - 0.5 * 0.284496736
        ) * t + 0.5 * 0.254829592
        tail = poly * t * bell
        below = jnp.where(pre >= 0.0, 1.0 - tail, tail)
        acts[:, at] = (pre * below).astype(BF)
        dpres[:, at] = (dact * (below + pre * bell * 0.3989422804014327)).astype(BF)
    act = acts[...]
    dpre = dpres[...]
    fc1_up_at = 3 * feats
    fc2_down_at = fc1_up_at + hidden
    fc2_up_at = fc2_down_at + hidden
    fc2_w = fc2_ref[...].reshape(hidden, feats)
    grad_reduced_fc1 = dot(fc1_up[...], dpre, NT).astype(BF)
    dlow = dot(dpre, fc1_ref[...].reshape(feats, hidden), NT) + dot(grad_reduced_fc1, fc1_down[...], TN)
    dx1 = dy.astype(F32) + norm_back(dlow, gain_ref[...], normed, inverse)
    branch = dx1.astype(BF)
    reduced_fc2 = dot(fc2_down[...], act, NT).astype(BF)
    total = (
        middle + fc2_bias_ref[...] + dot(act, fc2_w, NN) + dot(reduced_fc2, fc2_up[...], TN)
    ).astype(BF)
    grad_reduced_proj = dot(proj_up[...], branch, NT).astype(BF)
    dattn = (
        dot(branch, proj_w, NT) + dot(grad_reduced_proj, proj_down[...], TN)
    ).astype(BF)
    for e in range(per_clip):
        rows = slice(e * count, (e + 1) * count)
        act_ref[e] = total[rows]
        dx1_ref[e] = dx1[rows]
        dattn_ref[e] = dattn[rows]
    grad_ref[0, :, :feats] = dot(grad_reduced_proj, attn, NN)
    grad_ref[0, :, feats : 2 * feats] = dot(reduced_proj, branch, NN)
    grad_ref[0, :, 2 * feats : fc1_up_at] = dot(grad_reduced_fc1, low, NN)
    grad_ref[0, :, fc1_up_at:fc2_down_at] = dot(reduced_fc1, dpre, NN)
    grad_ref[0, :, fc2_down_at:fc2_up_at] = dot(grad_reduced_fc2, act, NN)
    grad_ref[0, :, fc2_up_at:] = dot(reduced_fc2, dy, NN)


PIECES = (
    (0, 0, 64),
    (0, 512, 192),
    (1, 0, 64),
    (1, 512, 64),
    (1, 1024, 64),
    (1, 5632, 64),
    (1, 1536, 256),
    (1, 3584, 256),
)


def gradient_rows(sources, part, j):
    halves = []
    for n in range(2):
        cells = []
        for array, start, width in PIECES:
            at = slice(start + j * width, start + (j + 1) * width)
            cells.append(sources[array][n, pl.ds(pl.multiple_of(part * 8, 8), 8), at])
        halves.append(jnp.concatenate(cells, axis=1))
    return jnp.concatenate(halves, axis=0)


def share_gradients(place, sources, ids_ref, refs, send, between):
    own, other, from_core, half, from_x, shares, from_clips, adapters, from_win, out = refs
    c, w, x, k = place.c, place.w, place.x, place.k
    clip_size = own.shape[0]
    for j in range(clip_size):
        other[j] = gradient_rows(sources, 1 - k, j).astype(BF)
    core_copy = send.copy(other, from_core, place.sibling)
    between[0]()
    for j in range(clip_size):
        own[j] = gradient_rows(sources, k, j)
    core_copy.wait_recv()
    own[...] += from_core[...].astype(F32)
    half[...] = own[:, :, pl.ds(pl.multiple_of((1 - x) * 512, 512), 512)].astype(BF)
    x_copy = send.copy(half, from_x, place.across)
    between[1]()
    x_copy.wait_recv()
    shares[...] = (
        own[:, :, pl.ds(pl.multiple_of(x * 512, 512), 512)] + from_x[...].astype(F32)
    ).astype(BF)
    from_clips[c] = shares[c]
    clip_copies = []
    for d in range(1, clip_size):
        to = (c + d) % clip_size
        clip_copies.append(send.copy(shares.at[to], from_clips.at[c], (to, w)))
    for copy in clip_copies:
        copy.wait_recv()
    for a in range(8):
        total = None
        for n in range(2 * clip_size):
            value = from_clips[n // 2].astype(F32)[8 * (n % 2) : 8 * (n % 2) + 8]
            value = jnp.where(ids_ref[n : n + 1, :] == float(a), value, 0.0)
            total = value if total is None else total + value
        adapters[a // 2, 8 * (a % 2) : 8 * (a % 2) + 8, :] = total
    from_win[w] = adapters[w]
    win_copies = []
    for d in range(1, 4):
        to = (w + d) % 4
        win_copies.append(send.copy(adapters.at[to], from_win.at[w], (c, to)))
    between[2]()
    for copy in win_copies:
        copy.wait_recv()
    for x2 in range(2):
        for k2 in range(2):
            for a in range(2):
                out[a, 8 * k2 : 8 * k2 + 8, 512 * x2 : 512 * x2 + 512] = from_win[
                    2 * x2 + k2, 8 * a : 8 * a + 8, :
                ]
    for copy in [core_copy, x_copy, *clip_copies, *win_copies]:
        copy.wait_send()


def attend_back_kernel(
    x_ref,
    gain_ref,
    weight_ref,
    down_ref,
    up_ref,
    probs_ref,
    attn_ref,
    qkv_ref,
    reduced_ref,
    dattn_ref,
    dx1_ref,
    *refs,
    scale,
    per_group,
    width,
    per_clip,
    remote_size,
):
    if remote_size:
        act_ref, grad_dense_ref, ids_ref, act_out_ref, dx_out_ref, sums_ref, *refs = refs
    else:
        dx_ref, grad_ref, *refs = refs
    values, keys_t, inner, dqkv, dquery_t, *refs = refs
    group = pl.program_id(1)
    groups = pl.num_programs(1)
    item = pl.program_id(0)
    step = item * groups + group
    if remote_size:
        items = act_ref.shape[0]
        place = Place(remote_size)
        act_rows = Rows(place, act_ref, *refs[:5])
        dx_own = refs[5]
        dx_rows = Rows(place, *refs[5:11])
        grad_ref = refs[11]
        share_refs, sems = refs[12:21], refs[21:]

        @pl.when(step == 0)
        def _():
            enter(
                [(place.c, (place.w + d) % 4) for d in range(1, 4)]
                + [((place.c + d) % remote_size, place.w) for d in range(1, remote_size)]
            )
            for i in range(items):
                act_rows.begin(i)

        for i in range(items):

            @pl.when(step == i + 1)
            def _():
                act_rows.mix(i)

            if i < items - 1:

                @pl.when(step == (i + 1) * 4 + 1)
                def _():
                    dx_rows.mix(i)

        @pl.when(step == 4 * items - 3)
        def _():
            for i in range(0, items, 2):
                act_rows.end(act_out_ref, i)
            act_rows.drain()

    feats = x_ref.shape[-1]
    rows = x_ref.shape[1]

    @pl.when(group == 0)
    def _():
        keys_t[...] = qkv_ref[0, :, feats : 2 * feats].T
        lane = lane_ids((rows, 128))
        ones = jnp.where(lane % width < 2, 1.0, 0.0).astype(BF)
        source = lax.broadcasted_iota(jnp.int32, (128, 128), 0)
        target = lane_ids((128, 128))
        pick = jnp.where(
            (source // width == target // width) & (target % width < 2), 1.0, 0.0
        ).astype(BF)
        pick = jnp.concatenate([pick, pick], axis=0)
        for g in range(feats // 128):
            at = slice(128 * g, 128 * g + 128)
            values[:, 256 * g : 256 * g + 128] = qkv_ref[0, :, 2 * feats + 128 * g : 2 * feats + 128 * g + 128]
            values[:, 256 * g + 128 : 256 * g + 256] = ones
            product = dattn_ref[0, :, at].astype(F32) * attn_ref[0, :, at].astype(F32)
            high = product.astype(BF)
            rest = (product - high.astype(F32)).astype(BF)
            sums = dot(jnp.concatenate([high, rest], axis=1), pick, NN)
            coarse = sums.astype(BF)
            fine = (sums - coarse.astype(F32)).astype(BF)
            inner[:, at] = -jnp.where(lane % width == 0, coarse, fine)

    blocks = pl.ds(pl.multiple_of(group * 128, 128), 128)
    values_now = values[:, pl.ds(pl.multiple_of(group * 256, 256), 256)]
    dattn_now = dattn_ref[0, :, blocks]
    inner_now = inner[:, blocks]
    query_now = qkv_ref[0, :, blocks]
    head_of_lane = lane_ids((rows, 128)) // width
    zero = jnp.zeros((rows, 128), BF)
    dvalue = None
    dkey = None
    for h in range(per_group):
        mine = head_of_lane == h
        dattn_own = jnp.where(mine, dattn_now, zero)
        query_own = jnp.where(mine, query_now, zero)
        right = jnp.concatenate([dattn_own, jnp.where(mine, inner_now, zero)], axis=1)
        probs = probs_ref[0, h]
        dscore = probs * dot(values_now, right, NT).astype(BF)
        partial = dot(probs, dattn_own, NN)
        dvalue = partial if dvalue is None else dvalue + partial
        partial = dot(dscore, query_own, NN)
        dkey = partial if dkey is None else dkey + partial
        at = pl.ds(pl.multiple_of((group * per_group + h) * width, width), width)
        dquery_t[at, :] = (dot(keys_t[at, :], dscore, NN) * scale).astype(BF)
    dqkv[:, pl.ds(pl.multiple_of(2 * feats + group * 128, 128), 128)] = dvalue.astype(BF)
    dqkv[:, pl.ds(pl.multiple_of(feats + group * 128, 128), 128)] = (dkey * LN2).astype(BF)

    @pl.when(group == groups - 1)
    def _():
        first = pl.program_id(0) % per_clip == 0
        dqkv[:, :feats] = dquery_t[...].T
        dall = dqkv[...]
        normed, inverse = norm_stats(x_ref[0].astype(F32))
        low = (normed * gain_ref[...]).astype(BF)
        grad_reduced = dot(up_ref[0], dall, NT).astype(BF)
        slot = item // per_clip if remote_size else 0
        add_rows(grad_ref, slot, slice(feats, 4 * feats), dot(reduced_ref[0], dall, NN), first)
        add_rows(grad_ref, slot, slice(0, feats), dot(grad_reduced, low, NN), first)
        dlow = (dot(dall, weight_ref[...], NT) + dot(grad_reduced, down_ref[0], TN)).astype(BF)
        dx = (dx1_ref[0] + norm_back(dlow.astype(F32), gain_ref[...], normed, inverse)).astype(BF)
        if not remote_size:
            dx_ref[0] = dx
            return
        dx_own[item] = dx
        for i in range(items):

            @pl.when(item == i)
            def _():
                dx_rows.begin(i)

    if remote_size:

        @pl.when(step == 4 * items - 1)
        def _():
            share_gradients(
                place,
                (grad_ref, grad_dense_ref),
                ids_ref,
                (*share_refs, sums_ref),
                Sender(*sems),
                (
                    lambda: dx_rows.mix(items - 1),
                    lambda: None,
                    lambda: [dx_rows.end(dx_out_ref, i) for i in range(0, items, 2)],
                ),
            )
            dx_rows.drain()


def whole(shape):
    return pl.BlockSpec(shape, lambda *at: (0,) * len(shape), pipeline_mode=pl.Buffered(1))


def compute(first, dy, adapter_ids, vectors, later, per_clip, remote_size):
    if remote_size:
        heads = first[1].shape[0]
        x_shape, rank = dy.shape, 16
    else:
        x, qkv_w, qkv_down, qkv_up, table = first
        heads, rank = table.shape[0], qkv_down.shape[1]
    items, rows, feats = dy.shape
    width = feats // heads
    per_group = 128 // width
    groups = heads // per_group
    scale = width**-0.5
    hidden = 4 * feats
    clips = items // per_clip

    def item(shape):
        return pl.BlockSpec((1, *shape), lambda i, *rest: (i,) + (0,) * len(shape))

    item_ids = adapter_ids
    any_space = pl.BlockSpec(memory_space=pl.ANY)

    def of_clip(shape):
        return pl.BlockSpec((1, *shape), lambda i, *rest: (i // per_clip, 0, 0))

    sems = pltpu.SemaphoreType.DMA
    if remote_size:
        shape = jax.ShapeDtypeStruct
        adapters = 8
        padded = 56 * heads
        ids = jnp.pad(adapter_ids.astype(F32)[None], ((0, 0), (0, 126)))
        args = (*first, ids, *[v.reshape(1, -1) for v in vectors], dy, *later)
        arg_specs = [whole(a.shape) for a in args]
        sent_out = [
            shape(dy.shape, BF),
            shape((2, remote_size, 2, 768, 128), BF),
            shape(dy.shape, BF),
            shape((feats, 3 * feats), BF),
            *[shape((1, n), F32) for n in (feats, feats, feats, hidden, feats)],
            shape((2 * remote_size, 512), F32),
        ]
        sent_specs = [whole(a.shape) for a in sent_out]
        sent_specs[1] = any_space
        row_scratch = [
            pltpu.VMEM(dy.shape, BF),
            pltpu.VMEM(dy.shape, BF),
            pltpu.VMEM((items, TOP, feats), BF),
            sems((2 * items,)),
            sems((2 * items,)),
        ]
        sent_scratch = [
            pltpu.VMEM((1, 3 * feats), F32),
            pltpu.VMEM((adapters, rank, feats), BF),
            pltpu.VMEM((adapters, rank, 3 * feats), BF),
            pltpu.VMEM((64, 512), BF),
            pltpu.VMEM((8, 128), F32),
            pltpu.VMEM((768, 128), BF),
            pltpu.VMEM((2, remote_size, 2, 64, 512), BF),
            pltpu.VMEM((remote_size, 8, 128), F32),
            pltpu.VMEM((15 * heads, 176), BF),
            pltpu.VMEM((15, padded, 128), F32),
            pltpu.VMEM((padded, 15 * 128), BF),
            pltpu.VMEM((8 * 128, rows), BF),
            *row_scratch,
            *row_scratch,
            *[sems((Gather.COPIES,)) for _ in range(4)],
            sems((remote_size,)),
            sems((remote_size,)),
            sems,
        ]
    else:
        gain1, qkv_bias, proj_bias, gain2, fc1_bias, fc2_bias = vectors
        clip_ids = jnp.broadcast_to(adapter_ids.astype(F32)[:, None], (clips, 128))
        args = (x, gain1, qkv_w, qkv_bias, clip_ids, qkv_down, qkv_up, table)
        arg_specs = [item((rows, feats)), *[whole(a.shape) for a in args[1:7]], any_space]
        sent_out, sent_specs, sent_scratch = [], [], []

    probs, attn, qkv, reduced, down_own, up_own, *arrived = pl.pallas_call(
        functools.partial(
            attend_kernel,
            scale=scale,
            per_group=per_group,
            width=width,
            per_clip=per_clip,
            remote_size=remote_size,
        ),
        grid=(items, groups),
        in_specs=arg_specs,
        out_specs=[
            pl.BlockSpec((1, per_group, rows, rows), lambda i, g: (i, g, 0, 0)),
            item((rows, feats)),
            item((rows, 3 * feats)),
            item((rank, rows)),
            of_clip((rank, feats)),
            of_clip((rank, 3 * feats)),
            *sent_specs,
        ],
        scratch_shapes=[
            pltpu.VMEM((rows, 2 * feats), BF),
            pltpu.VMEM((rows, feats), BF),
            pltpu.VMEM((feats, rows), BF),
            pltpu.VMEM((feats, rows), BF),
            pltpu.VMEM((2, rows, rows), F32),
            pltpu.VMEM((heads, rows, rows), F32),
            sems((groups,)),
            pltpu.VMEM((rows, 128), BF),
            *sent_scratch,
        ],
        out_shape=[
            jax.ShapeDtypeStruct((items, heads, rows, rows), BF),
            jax.ShapeDtypeStruct((items, rows, feats), BF),
            jax.ShapeDtypeStruct((items, rows, 3 * feats), BF),
            jax.ShapeDtypeStruct((items, rank, rows), BF),
            jax.ShapeDtypeStruct((clips, rank, feats), BF),
            jax.ShapeDtypeStruct((clips, rank, 3 * feats), BF),
            *sent_out,
        ],
        compiler_params=pltpu.CompilerParams(
            vmem_limit_bytes=VMEM_LIMIT,
            dimension_semantics=("arbitrary", "arbitrary"),
            **({"collective_id": 2, "has_side_effects": True} if remote_size else {}),
        ),
        cost_estimate=pl.CostEstimate(flops=4 * 10**10, bytes_accessed=10**7, transcendentals=0),
        name="attend",
    )(*args)
    if remote_size:
        dy, staged, x, qkv_w, gain1, proj_bias, gain2, fc1_bias, fc2_bias, all_ids = arrived
    else:
        (staged,) = later

    span = 4 * feats + 2 * hidden
    def tile(n):
        def index(c, ids):
            return ids[c] // 2 % 2, 0, ids[c] // 4, 36 + 2 * n + ids[c] % 2, 0

        return pl.BlockSpec((1, 8, 1, rank, 128), index)

    def clip(array_shape):
        return pl.BlockSpec((per_clip, *array_shape[1:]), lambda c, ids: (c, 0, 0))

    chunk = 512
    act, dx1, dattn, grad_dense = pl.pallas_call(
        functools.partial(dense_kernel, per_clip=per_clip, chunk=chunk),
        grid_spec=pltpu.PrefetchScalarGridSpec(
            num_scalar_prefetch=1,
            grid=(clips,),
            in_specs=[
                clip(x.shape),
                clip(x.shape),
                whole(gain2.shape),
                whole(proj_bias.shape),
                whole(fc1_bias.shape),
                whole(fc2_bias.shape),
                clip(x.shape),
                any_space,
                *[tile(n) for n in range(6)],
            ],
            out_specs=[
                clip(x.shape),
                clip(x.shape),
                clip(x.shape),
                pl.BlockSpec((1, rank, span), lambda c, ids: (c, 0, 0)),
            ],
            scratch_shapes=[
                pltpu.VMEM((8, feats // 8, feats), BF),
                pltpu.VMEM((8, feats // 8, hidden), BF),
                pltpu.VMEM((8, hidden // 8, feats), BF),
                *[pltpu.VMEM((rank, n), BF) for n in (feats, feats, feats, hidden, hidden, feats)],
                pltpu.VMEM((2, per_clip * rows, chunk), F32),
                pltpu.VMEM((per_clip * rows, hidden), BF),
                pltpu.VMEM((per_clip * rows, hidden), BF),
                pltpu.SemaphoreType.DMA((24,)),
            ],
        ),
        out_shape=[
            jax.ShapeDtypeStruct((items, rows, feats), BF),
            jax.ShapeDtypeStruct((items, rows, feats), F32),
            jax.ShapeDtypeStruct((items, rows, feats), BF),
            jax.ShapeDtypeStruct((clips, rank, span), F32),
        ],
        compiler_params=pltpu.CompilerParams(
            vmem_limit_bytes=VMEM_LIMIT, dimension_semantics=("arbitrary",)
        ),
        cost_estimate=pl.CostEstimate(flops=5 * 10**10, bytes_accessed=10**7, transcendentals=0),
        name="dense",
    )(
        item_ids, x, attn, gain2, proj_bias, fc1_bias, fc2_bias, dy, staged, *([staged] * 6)
    )

    if remote_size:
        assert (clips, per_clip) == (2, 2)
        count = remote_size
        back_in = (act, grad_dense, all_ids)
        back_out = [whole(x.shape), whole(x.shape), whole((2, rank, 1024))]
        back_shape = [
            jax.ShapeDtypeStruct(x.shape, BF),
            jax.ShapeDtypeStruct(x.shape, BF),
            jax.ShapeDtypeStruct((2, rank, 1024), F32),
        ]
        back_scratch = [
            *row_scratch,
            pltpu.VMEM(x.shape, BF),
            *row_scratch,
            pltpu.VMEM((clips, rank, 4 * feats), F32),
            pltpu.VMEM((count, 16, 1024), F32),
            pltpu.VMEM((count, 16, 1024), BF),
            pltpu.VMEM((count, 16, 1024), BF),
            pltpu.VMEM((count, 16, 512), BF),
            pltpu.VMEM((count, 16, 512), BF),
            pltpu.VMEM((count, 16, 512), BF),
            pltpu.VMEM((count, 16, 512), BF),
            pltpu.VMEM((4, 16, 512), F32),
            pltpu.VMEM((4, 16, 512), F32),
            sems((16,)),
            sems((16,)),
        ]
    else:
        back_in, back_scratch = (), []
        back_out = [
            item((rows, feats)),
            pl.BlockSpec((1, rank, 4 * feats), lambda i, g: (i // per_clip, 0, 0)),
        ]
        back_shape = [
            jax.ShapeDtypeStruct((items, rows, feats), BF),
            jax.ShapeDtypeStruct((clips, rank, 4 * feats), F32),
        ]
    results = pl.pallas_call(
        functools.partial(
            attend_back_kernel,
            scale=scale,
            per_group=per_group,
            width=width,
            per_clip=per_clip,
            remote_size=remote_size,
        ),
        grid=(items, groups),
        in_specs=[
            item((rows, feats)),
            whole(gain1.shape),
            whole(qkv_w.shape),
            of_clip((rank, feats)),
            of_clip((rank, 3 * feats)),
            pl.BlockSpec((1, per_group, rows, rows), lambda i, g: (i, g, 0, 0)),
            item((rows, feats)),
            item((rows, 3 * feats)),
            item((rank, rows)),
            item((rows, feats)),
            item((rows, feats)),
            *[whole(a.shape) for a in back_in],
        ],
        out_specs=back_out,
        scratch_shapes=[
            pltpu.VMEM((rows, 2 * feats), BF),
            pltpu.VMEM((feats, rows), BF),
            pltpu.VMEM((rows, feats), BF),
            pltpu.VMEM((rows, 3 * feats), BF),
            pltpu.VMEM((feats, rows), BF),
            *back_scratch,
        ],
        out_shape=back_shape,
        compiler_params=pltpu.CompilerParams(
            vmem_limit_bytes=VMEM_LIMIT, dimension_semantics=("arbitrary", "arbitrary"),
            **({"collective_id": 1, "has_side_effects": True} if remote_size else {}),
        ),
        cost_estimate=pl.CostEstimate(flops=5 * 10**10, bytes_accessed=10**7, transcendentals=0),
        name="attend_back",
    )(x, gain1, qkv_w, down_own, up_own, probs, attn, qkv, reduced, dattn, dx1, *back_in)
    if remote_size:
        return results
    return (act, *results, grad_dense)


def exchange(x, win_size):
    local = x.shape[1]
    bits = local.bit_length() - 1
    at = jnp.arange(TOK)
    taken = (at // 49 < 4, at // 7 % 7 < 3, at % 7 < 3)
    for bit, rows in zip((2, 1, 0), taken):
        if bit < bits:
            split = x.reshape(x.shape[0], local >> (bit + 1), 2, 1 << bit, TOK, -1)
            other = jnp.flip(split, axis=2).reshape(x.shape)
        else:
            other = lax.ppermute(x, "win", [(i, i ^ 1 << bit - bits) for i in range(win_size)])
        x = jnp.where(rows[None, None, :, None], other, x)
    return x


def bias_by_pair(table):
    heads = table.shape[0]
    side = jnp.arange(49)
    high, wide = (side // 7 + 4) % 7, (side % 7 + 4) % 7
    offset = (high[None, :] - high[:, None] + 6) * 13 + wide[None, :] - wide[:, None] + 6
    pick = (jnp.arange(169)[:, None, None] == offset[None]).astype(BF)
    found = jnp.einsum(
        "mad,dkq->mkaq", table.reshape(heads, 15, 169), pick, preferred_element_type=F32
    )
    found = (found * LOG2E).reshape(heads, 49, 15 * 49)
    blocks = []
    for key_block in range(8):
        t = (key_block + 4) % 8
        blocks.append(
            jnp.concatenate(
                (found[..., (11 - t) * 49 : (15 - t) * 49], found[..., (7 - t) * 49 : (11 - t) * 49]),
                axis=-1,
            )
        )
    return jnp.stack(blocks, axis=1).reshape(heads, TOK, TOK)


def gather(array, spec):
    for axis, name in enumerate(spec):
        if name is not None:
            array = lax.all_gather(array, name, axis=axis, tiled=True)
    return array


def stage_whole(proj_w, fc1_w, fc2_w, maps):
    proj_down, proj_up, fc1_down, fc1_up, fc2_down, fc2_up = maps
    count = proj_down.shape[0]

    def short(a):
        return a.reshape(4, count // 4 * 16, 8, 64).transpose(2, 0, 1, 3)

    def long(a):
        return a.reshape(4, count // 4 * 16, 8, 2, 128).transpose(2, 0, 3, 1, 4).reshape(8, 4, -1, 128)

    return jnp.concatenate(
        (
            proj_w.reshape(8, 64, 4, 128).transpose(0, 2, 1, 3),
            fc1_w.reshape(8, 64, 4, 4, 128).transpose(0, 2, 3, 1, 4).reshape(8, 4, 256, 128),
            fc2_w.reshape(8, 256, 4, 128).transpose(0, 2, 1, 3),
            jnp.concatenate((short(proj_down), short(proj_up)), axis=-1),
            jnp.concatenate((short(fc1_down), short(fc2_up)), axis=-1),
            long(fc1_up),
            long(fc2_down),
        ),
        axis=2,
    )


def by_core(staged):
    return staged.reshape(8, 2, 2, *staged.shape[2:]).transpose(2, 0, 1, 3, 4)


def per_device(
    tokens, cotangent, adapter_ids, ln1_gain, qkv_weight, qkv_bias, proj_weight, proj_bias, ln2_gain,
    fc1_weight, fc1_bias, fc2_weight, fc2_bias, bias_table, qkv_down, qkv_up, proj_down, proj_up,
    fc1_down, fc1_up, fc2_down, fc2_up, *, clip_size, win_size,
):
    clips, local, rows, feats = tokens.shape
    items = clips * local
    heads = bias_table.shape[0]
    vecs = (ln1_gain, qkv_bias, proj_bias, ln2_gain, fc1_bias, fc2_bias)
    flat = (items, rows, feats)
    downs = [a.transpose(0, 2, 1) for a in (qkv_down, proj_down, fc1_down, fc2_down)]
    own_kernels = (clip_size, win_size, clips, local) == (8, 4, 2, 2)
    if own_kernels:
        first = (tokens.reshape(flat), bias_table, qkv_weight, downs[0], qkv_up)
        dy = cotangent.reshape(flat)
        vectors = vecs
        later = (proj_weight, fc1_weight, fc2_weight, downs[1], proj_up, downs[2], fc1_up, downs[3], fc2_up)
    else:
        grid2, by_down, by_up = ("clip", "win"), ("win", None, "clip"), ("win", None, "clip")
        maps = (downs[1], proj_up, downs[2], fc1_up, downs[3], fc2_up)
        staged = stage_whole(
            *[gather(a, grid2) for a in (proj_weight, fc1_weight, fc2_weight)],
            [gather(a, by_up) for a in maps],
        )
        later = (by_core(staged),)
        vectors = [gather(v, ("clip",)).reshape(1, -1).astype(F32) for v in vecs]
        first = (
            exchange(tokens, win_size).reshape(flat),
            gather(qkv_weight, grid2),
            gather(downs[0], by_down),
            gather(qkv_up, by_up),
            bias_by_pair(bias_table),
        )
        dy = exchange(cotangent, win_size).reshape(flat)
    results = compute(
        first, dy, adapter_ids, vectors, later, local, clip_size if own_kernels else 0
    )
    if own_kernels:
        act_out, dx_out, sums = results
        qd, qu, pd, pu, f1d, f2u, f1u, f2d = [
            sums[..., first:last]
            for first, last in zip(
                (0, 64, 256, 320, 384, 448, 512, 768), (64, 256, 320, 384, 448, 512, 768, 1024)
            )
        ]
        turned = [a.transpose(0, 2, 1) for a in (qd, pd, f1d, f2d)]
        return (
            act_out.reshape(tokens.shape), dx_out.reshape(tokens.shape),
            turned[0], qu, turned[1], pu, turned[2], f1u, turned[3], f2u,
        )
    act, dx, grad_qkv, grad_dense = results
    activations = exchange(act.reshape(tokens.shape), win_size)
    input_grad = exchange(dx.reshape(tokens.shape), win_size)
    adapter_count = win_size * qkv_down.shape[0]
    hot = (adapter_ids[:, None] == jnp.arange(adapter_count)[None]).astype(F32)
    hidden = fc1_weight.shape[1] * win_size
    spans = (feats, 3 * feats, feats, feats, feats, hidden, hidden, feats)
    grads = jnp.concatenate((grad_qkv, grad_dense), axis=-1)
    rank = grads.shape[1]
    parts, at = [], 0
    for span in spans:
        parts.append(
            grads[..., at : at + span].reshape(clips, rank, clip_size, span // clip_size)
        )
        at += span
    mine = jnp.concatenate(parts, axis=-1)
    grown = jnp.sum(hot[:, :, None, None, None] * mine[:, None], axis=0)
    grown = grown.transpose(2, 0, 1, 3).astype(BF)
    total = lax.psum_scatter(grown, "clip", scatter_dimension=0, tiled=True)[0]
    total = lax.psum_scatter(total, "win", scatter_dimension=0, tiled=True).astype(F32)
    outs, at = [], 0
    for n, span in enumerate(spans):
        width = span // clip_size
        part = total[..., at : at + width]
        at += width
        outs.append(part.transpose(0, 2, 1) if n % 2 == 0 else part)
    return (activations, input_grad, *outs)


def solution(mesh):
    split = P("clip", "win", None, None)
    grid2 = P("clip", "win")
    down = P("win", "clip", None)
    up = P("win", None, "clip")
    one = P("clip")
    return jax.shard_map(
        functools.partial(
            per_device, clip_size=mesh.shape["clip"], win_size=mesh.shape["win"]
        ),
        mesh=mesh,
        in_specs=(
            split, split, one, one, grid2, one, grid2, one, one, grid2, one, grid2, one, P(),
            down, up, down, up, down, up, down, up,
        ),
        out_specs=(split, split, down, up, down, up, down, up, down, up),
        check_vma=False,
    )
```

profile of v0, /device:TPU:0, one launch (start us, length us, event | category | flops | bytes accessed | tf_op | source)
XLA Modules:
  0.0 209.8 jit_solution(8377298543141436298)
XLA Ops:
  0.6 0.7 convert_bitcast_fusion
  1.3 0.5 pad.4.refs_5_
  1.8 1.2 reshape.52.refs_7_
  3.0 1.2 reshape.55.refs_10_
  4.3 81.7 %attend.1 = (bf16[4,16,392,392]{3,2,1,0:T(8,128)(2,1)}, bf16[4,392,512]{2,1,0:T(8,128)(2,1)}, bf16[4,392,1536]{2,1,0:T(8,128)(2,1)}, bf16[4,16,392]{2,1,0:T(8,12...) custom-call(bf16[4,392,512]{2,1,0:T(8,128)(2,1)} %bitcast.24, ...), custom_call_target="tpu_custom_call" | custom-call | flops 40000000000 | bytes 10000000 | tf_op jit(solution)/shard_map/attend/pallas_call | solution.py:1036
  85.9 40.2 %dense.1 = (bf16[4,392,512]{2,1,0:T(8,128)(2,1)}, f32[4,392,512]{2,1,0:T(8,128)}, bf16[4,392,512]{2,1,0:T(8,128)(2,1)}, f32[2,16,6144]{2,1,0:T(8,128)}) custom-call(s32[2]{0:T(128)} %ids_ref.1, bf16[4,392,512]{2,1,0:T(8,128)(2,1)} %get-tuple-element.33.x_ref, bf16[4,392,512]{2,1,0:T(8,128)(2,1)} %get-tuple-element.39.attn_ref, ...), custom_call_target="tpu_custom_call" | custom-call | flops 49999998976 | bytes 10000000 | tf_op jit(solution)/shard_map/dense/pallas_call | solution.py:1100
  126.2 75.3 %attend_back.1 = (bf16[4,392,512]{2,1,0:T(8,128)(2,1)}, bf16[4,392,512]{2,1,0:T(8,128)(2,1)}, f32[2,16,1024]{2,1,0:T(8,128)}) custom-call(bf16[4,392,512]{2,1,0:T(8,128)(2,1)} %get-tuple-element.33.x_ref, f32[1,512]{1,0:T(1,128)} %get-tuple-element.34.gain_ref, bf16[512,1536]{1,0:T(8,128)(2,1)} %get-tuple-element.35.weight_ref, ...), custom_call_target="tpu_custom_call" | custom-call | flops 49999998976 | bytes 10000000 | tf_op jit(solution)/shard_map/attend_back/pallas_call | solution.py:1185
  201.5 1.5 slice.25
  203.0 1.4 slice_bitcast_fusion
  204.4 1.5 fusion
  205.9 0.0 copy-start
  205.9 2.8 %copy.34 = bf16[2,2,392,512]{3,2,1,0:T(8,128)(2,1)} copy(bf16[2,2,392,512]{3,2,1,0:T(8,128)(2,1)} %bitcast.23) | data formatting | bytes 3211264
  208.7 0.0 copy-done
  208.7 1.2 copy.35
Async XLA Ops:
  205.9 2.8 %copy-start = (bf16[4,392,512]{2,1,0:T(8,128)(2,1)S(1)}, bf16[4,392,512]{2,1,0:T(8,128)(2,1)}, u32[]{:S(2)}) copy-start(bf16[4,392,512]{2,1,0:T(8,128)(2,1)} %get-tuple-element.54) | copy-start | bytes 4816900
where the time goes:
time: 210 us
  Pallas kernels  197 us (94%)
  local copies, waits for them, and re-layouts  11.3 us (5%)
    pallas_call x1, Pallas kernels, compute(): pl.pallas_call(functools.partial(attend_kernel, scale=scale, per_group=pe...  81.7 us
    pallas_call x1, Pallas kernels, compute(): pl.pallas_call(functools.partial(attend_back_kernel, scale=scale, per_gro...  75.3 us
    pallas_call x1, Pallas kernels, compute(): pl.pallas_call(functools.partial(dense_kernel, per_clip=per_clip, chunk=c...  40.2 us

commit v1 on v0

--- a/solution.py
+++ b/solution.py
@@ -266,7 +266,8 @@
     vec[3:4, :] = f1b_ref[:, 0:128].astype(F32)
     vec[4:5, :] = f1b_ref[:, 128:256].astype(F32)
     vec[5:6, 0:64] = f2b_ref[...].astype(F32)
-    vec[5:6, 64:128] = ids_ref[:, 0:64]
+    vec[5:6, 64:128] = jnp.zeros((1, 64), F32)
+    vec[5:6, 64:66] = ids_ref[...].astype(F32)
     vec[6:8, :] = jnp.zeros((2, 128), F32)
 
 
@@ -462,13 +463,13 @@
             def _():
                 x_rows.end(x_ref, n)
 
-        for t, at in enumerate((4, 8, 11)):
+        for t, at in enumerate((4, 8, 12)):
 
             @pl.when(step == at)
             def _():
                 gather2.from_z(t)
 
-        for t, at in ((-1, 5), (0, 9), (1, 12), (2, 15)):
+        for t, at in ((-1, 5), (0, 9), (1, 13), (2, 15)):
 
             @pl.when(step == at)
             def _():
@@ -734,15 +735,21 @@
 )
 
 
-def gradient_rows(sources, part, j):
+def gradient_rows(sources, part, j, pieces):
     halves = []
     for n in range(2):
         cells = []
-        for array, start, width in PIECES:
+        for array, start, width in pieces:
             at = slice(start + j * width, start + (j + 1) * width)
             cells.append(sources[array][n, pl.ds(pl.multiple_of(part * 8, 8), 8), at])
         halves.append(jnp.concatenate(cells, axis=1))
     return jnp.concatenate(halves, axis=0)
+
+
+def early_gradients(place, sources, own, other):
+    for j in range(own.shape[0]):
+        own[j, :, 256:] = gradient_rows(sources, place.k, j, PIECES[2:])
+        other[j, :, 256:] = gradient_rows(sources, 1 - place.k, j, PIECES[2:]).astype(BF)
 
 
 def share_gradients(place, sources, ids_ref, refs, send, between):
@@ -750,11 +757,11 @@
     c, w, x, k = place.c, place.w, place.x, place.k
     clip_size = own.shape[0]
     for j in range(clip_size):
-        other[j] = gradient_rows(sources, 1 - k, j).astype(BF)
+        other[j, :, 0:256] = gradient_rows(sources, 1 - k, j, PIECES[:2]).astype(BF)
     core_copy = send.copy(other, from_core, place.sibling)
     between[0]()
     for j in range(clip_size):
-        own[j] = gradient_rows(sources, k, j)
+        own[j, :, 0:256] = gradient_rows(sources, k, j, PIECES[:2])
     core_copy.wait_recv()
     own[...] += from_core[...].astype(F32)
     half[...] = own[:, :, pl.ds(pl.multiple_of((1 - x) * 512, 512), 512)].astype(BF)
@@ -854,6 +861,10 @@
                 def _():
                     dx_rows.mix(i)
 
+        @pl.when(step == 6)
+        def _():
+            early_gradients(place, (None, grad_dense_ref), share_refs[0], share_refs[1])
+
         @pl.when(step == 4 * items - 3)
         def _():
             for i in range(0, items, 2):
@@ -945,8 +956,8 @@
                 (*share_refs, sums_ref),
                 Sender(*sems),
                 (
+                    lambda: None,
                     lambda: dx_rows.mix(items - 1),
-                    lambda: None,
                     lambda: [dx_rows.end(dx_out_ref, i) for i in range(0, items, 2)],
                 ),
             )
@@ -986,7 +997,7 @@
         shape = jax.ShapeDtypeStruct
         adapters = 8
         padded = 56 * heads
-        ids = jnp.pad(adapter_ids.astype(F32)[None], ((0, 0), (0, 126)))
+        ids = adapter_ids[None]
         args = (*first, ids, *[v.reshape(1, -1) for v in vectors], dy, *later)
         arg_specs = [whole(a.shape) for a in args]
         sent_out = [

time: 210 us -> 204 us (0.971)
  Pallas kernels: 197 us -> 192 us
    pallas_call x1, Pallas kernels: 75.3 us -> 69.8 us  [compute(): pl.pallas_call(functools.partial(attend_back_kernel, scale=scale, per_gro...]
where the time goes in v1:
time: 204 us; the launch traced here: 203 us
  Pallas kernels  192 us (94%)
  local copies, waits for them, and re-layouts  10.8 us (5%)
    pallas_call x1, Pallas kernels, compute(): pl.pallas_call(functools.partial(attend_kernel, scale=scale, per_group=pe...  82 us
    pallas_call x1, Pallas kernels, compute(): pl.pallas_call(functools.partial(attend_back_kernel, scale=scale, per_gro...  69.8 us
    pallas_call x1, Pallas kernels, compute(): pl.pallas_call(functools.partial(dense_kernel, per_clip=per_clip, chunk=c...  40.2 us

profile of v1, /device:TPU:0, one launch (start us, length us, event | category | flops | bytes accessed | tf_op | source)
XLA Modules:
  0.0 203.5 jit_solution(15241857245990751465)
XLA Ops:
  0.6 1.2 reshape.52.refs_7_
  1.9 1.2 reshape.55.refs_10_
  3.1 82.0 %attend.1 = (bf16[4,16,392,392]{3,2,1,0:T(8,128)(2,1)}, bf16[4,392,512]{2,1,0:T(8,128)(2,1)}, bf16[4,392,1536]{2,1,0:T(8,128)(2,1)}, bf16[4,16,392]{2,1,0:T(8,12...) custom-call(bf16[4,392,512]{2,1,0:T(8,128)(2,1)} %bitcast.23, ...), custom_call_target="tpu_custom_call" | custom-call | flops 40000000000 | bytes 10000000 | tf_op jit(solution)/shard_map/attend/pallas_call | solution.py:1047
  85.1 40.2 %dense.1 = (bf16[4,392,512]{2,1,0:T(8,128)(2,1)}, f32[4,392,512]{2,1,0:T(8,128)}, bf16[4,392,512]{2,1,0:T(8,128)(2,1)}, f32[2,16,6144]{2,1,0:T(8,128)}) custom-call(s32[2]{0:T(128)} %ids_ref.1, bf16[4,392,512]{2,1,0:T(8,128)(2,1)} %get-tuple-element.33.x_ref, bf16[4,392,512]{2,1,0:T(8,128)(2,1)} %get-tuple-element.39.attn_ref, ...), custom_call_target="tpu_custom_call" | custom-call | flops 49999998976 | bytes 10000000 | tf_op jit(solution)/shard_map/dense/pallas_call | solution.py:1111
  125.3 69.8 %attend_back.1 = (bf16[4,392,512]{2,1,0:T(8,128)(2,1)}, bf16[4,392,512]{2,1,0:T(8,128)(2,1)}, f32[2,16,1024]{2,1,0:T(8,128)}) custom-call(bf16[4,392,512]{2,1,0:T(8,128)(2,1)} %get-tuple-element.33.x_ref, f32[1,512]{1,0:T(1,128)} %get-tuple-element.34.gain_ref, bf16[512,1536]{1,0:T(8,128)(2,1)} %get-tuple-element.35.weight_ref, ...), custom_call_target="tpu_custom_call" | custom-call | flops 49999998976 | bytes 10000000 | tf_op jit(solution)/shard_map/attend_back/pallas_call | solution.py:1196
  195.1 1.5 slice.25
  196.6 1.4 slice_bitcast_fusion
  198.0 1.5 fusion
  199.5 0.0 copy-start
  199.5 2.8 %copy.34 = bf16[2,2,392,512]{3,2,1,0:T(8,128)(2,1)} copy(bf16[2,2,392,512]{3,2,1,0:T(8,128)(2,1)} %bitcast.22) | data formatting | bytes 3211264
  202.3 0.0 copy-done
  202.3 1.2 copy.35
Async XLA Ops:
  199.5 2.8 %copy-start = (bf16[4,392,512]{2,1,0:T(8,128)(2,1)S(1)}, bf16[4,392,512]{2,1,0:T(8,128)(2,1)}, u32[]{:S(2)}) copy-start(bf16[4,392,512]{2,1,0:T(8,128)(2,1)} %get-tuple-element.54) | copy-start | bytes 4816900

commit v2 on v1

--- a/solution.py
+++ b/solution.py
@@ -906,13 +906,21 @@
     zero = jnp.zeros((rows, 128), BF)
     dvalue = None
     dkey = None
-    for h in range(per_group):
+
+    def dprobs_of(h):
         mine = head_of_lane == h
         dattn_own = jnp.where(mine, dattn_now, zero)
-        query_own = jnp.where(mine, query_now, zero)
         right = jnp.concatenate([dattn_own, jnp.where(mine, inner_now, zero)], axis=1)
+        return dattn_own, dot(values_now, right, NT).astype(BF)
+
+    ready = dprobs_of(0)
+    for h in range(per_group):
+        dattn_own, dprobs = ready
+        if h + 1 < per_group:
+            ready = dprobs_of(h + 1)
+        query_own = jnp.where(head_of_lane == h, query_now, zero)
         probs = probs_ref[0, h]
-        dscore = probs * dot(values_now, right, NT).astype(BF)
+        dscore = probs * dprobs
         partial = dot(probs, dattn_own, NN)
         dvalue = partial if dvalue is None else dvalue + partial
         partial = dot(dscore, query_own, NN)

time: 204 us -> 202 us (level)
  no operation moved by 1% of the time
where the time goes in v2:
time: 202 us; the launch traced here: 201 us
  Pallas kernels  190 us (94%)
  local copies, waits for them, and re-layouts  10.8 us (5%)
    pallas_call x1, Pallas kernels, compute(): pl.pallas_call(functools.partial(attend_kernel, scale=scale, per_group=pe...  82 us
    pallas_call x1, Pallas kernels, compute(): pl.pallas_call(functools.partial(attend_back_kernel, scale=scale, per_gro...  67.9 us
    pallas_call x1, Pallas kernels, compute(): pl.pallas_call(functools.partial(dense_kernel, per_clip=per_clip, chunk=c...  40.2 us

profile of v2, /device:TPU:0, one launch (start us, length us, event | category | flops | bytes accessed | tf_op | source)
XLA Modules:
  0.0 201.5 jit_solution(4755614602688324098)
XLA Ops:
  0.6 1.2 reshape.52.refs_7_
  1.9 1.2 reshape.55.refs_10_
  3.1 82.0 %attend.1 = (bf16[4,16,392,392]{3,2,1,0:T(8,128)(2,1)}, bf16[4,392,512]{2,1,0:T(8,128)(2,1)}, bf16[4,392,1536]{2,1,0:T(8,128)(2,1)}, bf16[4,16,392]{2,1,0:T(8,12...) custom-call(bf16[4,392,512]{2,1,0:T(8,128)(2,1)} %bitcast.23, ...), custom_call_target="tpu_custom_call" | custom-call | flops 40000000000 | bytes 10000000 | tf_op jit(solution)/shard_map/attend/pallas_call | solution.py:1055
  85.1 40.2 %dense.1 = (bf16[4,392,512]{2,1,0:T(8,128)(2,1)}, f32[4,392,512]{2,1,0:T(8,128)}, bf16[4,392,512]{2,1,0:T(8,128)(2,1)}, f32[2,16,6144]{2,1,0:T(8,128)}) custom-call(s32[2]{0:T(128)} %ids_ref.1, bf16[4,392,512]{2,1,0:T(8,128)(2,1)} %get-tuple-element.33.x_ref, bf16[4,392,512]{2,1,0:T(8,128)(2,1)} %get-tuple-element.39.attn_ref, ...), custom_call_target="tpu_custom_call" | custom-call | flops 49999998976 | bytes 10000000 | tf_op jit(solution)/shard_map/dense/pallas_call | solution.py:1119
  125.3 67.9 %attend_back.1 = (bf16[4,392,512]{2,1,0:T(8,128)(2,1)}, bf16[4,392,512]{2,1,0:T(8,128)(2,1)}, f32[2,16,1024]{2,1,0:T(8,128)}) custom-call(bf16[4,392,512]{2,1,0:T(8,128)(2,1)} %get-tuple-element.33.x_ref, f32[1,512]{1,0:T(1,128)} %get-tuple-element.34.gain_ref, bf16[512,1536]{1,0:T(8,128)(2,1)} %get-tuple-element.35.weight_ref, ...), custom_call_target="tpu_custom_call" | custom-call | flops 49999998976 | bytes 10000000 | tf_op jit(solution)/shard_map/attend_back/pallas_call | solution.py:1204
  193.2 1.5 slice.25
  194.6 1.4 slice_bitcast_fusion
  196.0 1.5 fusion
  197.5 0.0 copy-start
  197.5 2.8 %copy.34 = bf16[2,2,392,512]{3,2,1,0:T(8,128)(2,1)} copy(bf16[2,2,392,512]{3,2,1,0:T(8,128)(2,1)} %bitcast.22) | data formatting | bytes 3211264
  200.3 0.0 copy-done
  200.3 1.2 copy.35
Async XLA Ops:
  197.5 2.8 %copy-start = (bf16[4,392,512]{2,1,0:T(8,128)(2,1)S(1)}, bf16[4,392,512]{2,1,0:T(8,128)(2,1)}, u32[]{:S(2)}) copy-start(bf16[4,392,512]{2,1,0:T(8,128)(2,1)} %get-tuple-element.54) | copy-start | bytes 4816900
